TPU v7x, 32 devices: a whole 2x2x4 slice. The times are simulated.
32 devices in a mesh: expert: 8 (over z, x), tensor: 4 (over y, core).
Axes of the slice: x: 2, y: 2, z: 4, core: 2. Of those that a mesh axis runs over, the one named last changes fastest.
Arguments:
- tokens: bfloat16 [512, 3072], P('expert', 'tensor'), may hold values from -6 to 6
- grad_out: bfloat16 [512, 3072], P('expert', 'tensor'), may hold values from -3 to 3
- probs: bfloat16 [512, 4], P('expert'), may hold values from 0.049804688 to 0.5
- routes: int32 [512, 4], P('expert'), may hold values from 0 to 7, all different within a row; in each aligned block of 64 rows (0 to 63, 64 to 127, ...) at most 40 rows name the same one
- gate_weight: bfloat16 [8, 5376, 3072], P('expert', 'tensor'), may hold values from -0.109375 to 0.109375
- up_weight: bfloat16 [8, 5376, 3072], P('expert', 'tensor'), may hold values from -0.109375 to 0.109375
- down_weight: bfloat16 [8, 5376, 3072], P('expert', 'tensor'), may hold values from -0.078125 to 0.078125
Outputs:
- d_tokens: bfloat16 [512, 3072], P('expert', 'tensor')
- d_probs: float32 [512, 4], P('expert')
- d_down: bfloat16 [8, 5376, 3072], P('expert', 'tensor')
Inputs may be any that keep to these rules, and one draw needn't show every extreme that they name: Each token's 4 experts differ. Among the 64 tokens of one index of expert, no expert is named by more than 40 routes, a bound that some block reaches of them.
All inputs are finite; a program needn't handle non-finite values.
Results may differ from a plain program's by a relative error of at most 0.007.
Values may be sent and summed in bfloat16 or wider, within the bound.
A program may use at most 128 MiB of HBM per device.

v0:
```python
import functools

import jax
import jax.numpy as jnp
from jax import lax
from jax.experimental import pallas as pl
from jax.experimental.pallas import tpu as pltpu
from jax.sharding import PartitionSpec as P

TOK_DEV = 64
SLOTS = 320
MESH_ID = pl.DeviceIdType.MESH
VMEM = pltpu.VMEM


def greet(peers):
    barrier = pltpu.get_barrier_semaphore()
    for peer in peers:
        pl.semaphore_signal(barrier, inc=1, device_id=peer, device_id_type=MESH_ID)
    pl.semaphore_wait(barrier, len(peers))


def remote(src, dst, send_sem, recv_sem, peer):
    return pltpu.make_async_remote_copy(
        src_ref=src,
        dst_ref=dst,
        send_sem=send_sem,
        recv_sem=recv_sem,
        device_id=peer,
        device_id_type=MESH_ID,
    )


def flip(index, bit):
    if bit == 0:
        return index
    return index + bit - 2 * bit * lax.rem(index // bit, 2)


def flip_all(index, number):
    for bit in (1, 2, 4, 8):
        if number & bit:
            index = flip(index, bit)
    return index


def dispatch_kernel(
    n, send_ref, probs_ref, x_ref, dy_ref, got_probs_ref,
    rows, own_sem, out_send, out_recv, core_send, core_recv,
    side_send, side_recv, pass_send, pass_recv, prob_send, prob_recv,
):
    e = lax.axis_index("expert")
    t = lax.axis_index("tensor")
    width = send_ref.shape[2]
    cap = send_ref.shape[1] // 2
    core, side, far = flip(t, 1), flip(t, 2), flip(flip(t, 1), 2)
    others = [flip_all(e, j) for j in range(n)]
    greet([(o, t) for o in others[1:]] + [(e, core), (e, side)])

    def columns(index):
        return pl.ds(pl.multiple_of(index * width, 128), width)

    mine = [
        remote(send_ref.at[others[j]], rows.at[e, :, columns(t)], out_send.at[j], out_recv.at[j], (others[j], t))
        for j in range(1, n)
    ]
    small = [
        remote(probs_ref.at[others[j]], got_probs_ref.at[e], prob_send.at[j], prob_recv.at[j], (others[j], t))
        for j in range(1, n)
    ]
    own = pltpu.make_async_copy(send_ref.at[e], rows.at[e, :, columns(t)], own_sem.at[0])
    own_probs = pltpu.make_async_copy(probs_ref.at[e], got_probs_ref.at[e], own_sem.at[1])
    own.start()
    own_probs.start()
    for copy in mine:
        copy.start()
    for copy in small:
        copy.start()

    def block(j, index):
        return rows.at[others[j], :, columns(index)]

    to_core = [remote(block(j, t), block(j, t), core_send.at[j], core_recv.at[j], (e, core)) for j in range(n)]
    to_side = [remote(block(j, t), block(j, t), side_send.at[j], side_recv.at[j], (e, side)) for j in range(n)]
    passed = [remote(block(j, side), block(j, side), pass_send.at[j], pass_recv.at[j], (e, core)) for j in range(n)]
    lag = 2
    for j in range(n + lag):
        if j < n:
            if j == 0:
                own.wait()
            else:
                remote(send_ref.at[others[j]], block(j, t), out_send.at[j], out_recv.at[j], (others[j], t)).wait_recv()
            to_side[j].start()
            to_core[j].start()
        if j >= lag:
            k = j - lag
            remote(block(k, side), block(k, side), side_send.at[k], side_recv.at[k], (e, side)).wait_recv()
            passed[k].start()
    own_probs.wait()
    for j in range(1, n):
        remote(
            probs_ref.at[others[j]], got_probs_ref.at[others[j]], prob_send.at[j], prob_recv.at[j], (others[j], t)
        ).wait_recv()
    for j in range(n):
        remote(block(j, core), block(j, core), core_send.at[j], core_recv.at[j], (e, core)).wait_recv()
        remote(block(j, far), block(j, far), pass_send.at[j], pass_recv.at[j], (e, core)).wait_recv()
    for k in range(n // 2):
        for q in range(x_ref.shape[1] // width):
            cols = slice(q * width, (q + 1) * width)
            first = rows[2 * k, :, cols].astype(jnp.float32)
            second = rows[2 * k + 1, :, cols].astype(jnp.float32)
            span = slice(2 * k * cap, 2 * (k + 1) * cap)
            x_ref[span, cols] = jnp.concatenate([first[:cap], second[:cap]], axis=0).astype(jnp.bfloat16)
            dy_ref[span, cols] = jnp.concatenate([first[cap:], second[cap:]], axis=0).astype(jnp.bfloat16)
    for copy in mine + small + to_core + to_side + passed:
        copy.wait_send()


def dispatch(send, probs):
    n, double, width = send.shape
    tensor = lax.axis_size("tensor")
    slots = n * double // 2
    full = width * tensor
    dma = pltpu.SemaphoreType.DMA
    return pl.pallas_call(
        functools.partial(dispatch_kernel, n),
        out_shape=(
            jax.ShapeDtypeStruct((slots, full), jnp.bfloat16),
            jax.ShapeDtypeStruct((slots, full), jnp.bfloat16),
            jax.ShapeDtypeStruct(probs.shape, jnp.float32),
        ),
        in_specs=[pl.BlockSpec(memory_space=VMEM)] * 2,
        out_specs=[pl.BlockSpec(memory_space=VMEM)] * 3,
        scratch_shapes=[pltpu.VMEM((n, double, full), jnp.bfloat16), dma((2,))] + [dma((n,))] * 10,
        compiler_params=pltpu.CompilerParams(
            collective_id=0, has_side_effects=True, vmem_limit_bytes=40 * 1024 * 1024
        ),
        cost_estimate=pl.CostEstimate(flops=0, bytes_accessed=slots * full * 8, transcendentals=0),
    )(send, probs)


def combine_kernel(
    n, gate_ref, up_ref, score_ref, w_gate, w_up, got_ref, got_score_ref,
    weights, keep, ship, from_core, mid, from_side, out, score_parts, score_sum,
    load_sem, core_send, core_recv, side_send, side_recv, out_send, out_recv, own_sem,
    sum_send, sum_recv, score_send, score_recv,
):
    e = lax.axis_index("expert")
    t = lax.axis_index("tensor")
    core, side, far = flip(t, 1), flip(t, 2), flip(flip(t, 1), 2)
    others = [flip_all(e, j) for j in range(n)]
    chunks, chunk, width = mid.shape
    cap = chunk // 2
    half = out.shape[2]
    quarters = (far, side, core, t)
    loads = []
    for i, quarter in enumerate(quarters):
        cols = pl.ds(pl.multiple_of(quarter * width, 128), width)
        for m, weight in enumerate((w_gate, w_up)):
            copy = pltpu.make_async_copy(weight.at[:, cols], weights.at[i, m], load_sem.at[i, m])
            copy.start()
            loads.append(copy)
    greet([(o, t) for o in others[1:]] + [(e, core), (e, side), (e, far)])
    sums = [
        remote(score_ref, score_parts.at[i], sum_send.at[i], sum_recv.at[i], (e, peer))
        for i, peer in enumerate((core, side, far))
    ]
    for copy in sums:
        copy.start()

    def product(i, dst):
        loads[2 * i].wait()
        loads[2 * i + 1].wait()

        @pl.loop(0, width // 256)
        def _(c):
            cols = pl.ds(pl.multiple_of(c * 256, 256), 256)
            dst[:, cols] = (
                jnp.dot(gate_ref[...], weights[i, 0, :, cols], preferred_element_type=jnp.float32)
                + jnp.dot(up_ref[...], weights[i, 1, :, cols], preferred_element_type=jnp.float32)
            ).astype(dst.dtype)

    def span(k):
        return pl.ds(pl.multiple_of(k * chunk, chunk), chunk)

    turns = (2, 3, 1, 0)
    pairs = [flip_all(e // 2, j) for j in range(chunks)]

    def give(i):
        copies = {}
        for j in turns:
            copies[j] = remote(
                ship.at[i, span(pairs[j])], from_core.at[i, j], core_send.at[i, j], core_recv.at[i, j], (e, core)
            )
            copies[j].start()
        return copies

    product(0, ship.at[0])
    give_far = give(0)
    product(1, keep.at[0])
    to_side = {}
    for j in turns:
        give_far[j].wait_recv()
        mid[j] = (keep[0, span(pairs[j]), :] + from_core[0, j].astype(jnp.float32)).astype(jnp.bfloat16)
        to_side[j] = remote(mid.at[j], from_side.at[j], side_send.at[j], side_recv.at[j], (e, side))
        to_side[j].start()
    product(2, ship.at[1])
    give_core = give(1)
    for copy in sums:
        copy.wait_recv()
    score_sum[...] = score_ref[...] + score_parts[0] + score_parts[1] + score_parts[2]
    own_score = pltpu.make_async_copy(score_sum.at[e], got_score_ref.at[e], own_sem.at[1])
    own_score.start()
    sent = []
    for j in range(1, n):
        copy = remote(
            score_sum.at[others[j]], got_score_ref.at[e], score_send.at[j], score_recv.at[j], (others[j], t)
        )
        copy.start()
        sent.append(copy)
    product(3, keep.at[1])
    own = pltpu.make_async_copy(out.at[0], got_ref.at[e], own_sem.at[0])
    for j in turns:
        give_core[j].wait_recv()
        to_side[j].wait_recv()
        total = (
            keep[1, span(pairs[j]), :] + from_core[1, j].astype(jnp.float32) + from_side[j].astype(jnp.float32)
        )
        low = jnp.concatenate([total[:cap, :half], total[:cap, half:]], axis=0).astype(jnp.bfloat16)
        high = jnp.concatenate([total[cap:, :half], total[cap:, half:]], axis=0).astype(jnp.bfloat16)
        odd = lax.rem(e, 2) == 1
        out[2 * j] = jnp.where(odd, high, low)
        out[2 * j + 1] = jnp.where(odd, low, high)
        for i in (2 * j, 2 * j + 1):
            if i == 0:
                own.start()
            else:
                copy = remote(out.at[i], got_ref.at[e], out_send.at[i], out_recv.at[i], (others[i], t))
                copy.start()
                sent.append(copy)
    own.wait()
    own_score.wait()
    for j in range(1, n):
        remote(out.at[j], got_ref.at[others[j]], out_send.at[j], out_recv.at[j], (others[j], t)).wait_recv()
        remote(
            score_sum.at[others[j]], got_score_ref.at[others[j]], score_send.at[j], score_recv.at[j], (others[j], t)
        ).wait_recv()
    for copy in list(give_far.values()) + list(give_core.values()) + sums + list(to_side.values()) + sent:
        copy.wait_send()


def combine(grad_gate, grad_up, scores, w_gate, w_up):
    tensor = lax.axis_size("tensor")
    slots, hidden = grad_gate.shape
    width = w_gate.shape[1] // tensor
    n = scores.shape[0]
    cap = slots // n
    chunk = 2 * cap
    dma = pltpu.SemaphoreType.DMA
    return pl.pallas_call(
        functools.partial(combine_kernel, n),
        out_shape=(
            jax.ShapeDtypeStruct((n, chunk, width // 2), jnp.bfloat16),
            jax.ShapeDtypeStruct(scores.shape, jnp.float32),
        ),
        in_specs=[pl.BlockSpec(memory_space=VMEM)] * 3 + [pl.BlockSpec(memory_space=pl.ANY)] * 2,
        out_specs=[pl.BlockSpec(memory_space=VMEM)] * 2,
        scratch_shapes=[
            pltpu.VMEM((tensor, 2, hidden, width), jnp.bfloat16),
            pltpu.VMEM((2, slots, width), jnp.float32),
            pltpu.VMEM((2, slots, width), jnp.bfloat16),
            pltpu.VMEM((2, n // 2, chunk, width), jnp.bfloat16),
            pltpu.VMEM((n // 2, chunk, width), jnp.bfloat16),
            pltpu.VMEM((n // 2, chunk, width), jnp.bfloat16),
            pltpu.VMEM((n, chunk, width // 2), jnp.bfloat16),
            pltpu.VMEM((3,) + scores.shape, jnp.float32),
            pltpu.VMEM(scores.shape, jnp.float32),
            dma((tensor, 2)),
            dma((2, n // 2)), dma((2, n // 2)),
            dma((n // 2,)), dma((n // 2,)),
            dma((n,)), dma((n,)), dma((2,)),
            dma((3,)), dma((3,)),
            dma((n,)), dma((n,)),
        ],
        compiler_params=pltpu.CompilerParams(
            collective_id=1, has_side_effects=True, vmem_limit_bytes=50 * 1024 * 1024
        ),
        cost_estimate=pl.CostEstimate(
            flops=4 * slots * hidden * width * tensor, bytes_accessed=4 * hidden * width * tensor, transcendentals=0
        ),
    )(grad_gate, grad_up, scores, w_gate, w_up)


def expert_grads(rows_x, rows_dy, prob_rows, w_gate, w_up, w_down):
    contract_last = (((1,), (1,)), ((), ()))
    pre_gate = lax.dot_general(rows_x, w_gate, contract_last, preferred_element_type=jnp.float32)
    pre_up = lax.dot_general(rows_x, w_up, contract_last, preferred_element_type=jnp.float32)
    sigmoid_a = jax.nn.sigmoid(pre_gate)
    silu_a = pre_gate * sigmoid_a
    hidden = (silu_a * pre_up).astype(jnp.bfloat16)
    back_hidden = lax.dot_general(rows_dy, w_down, contract_last, preferred_element_type=jnp.float32)
    score_part = jnp.sum(hidden.astype(jnp.float32) * back_hidden, axis=1)
    scaled_hidden = (prob_rows[:, None] * hidden.astype(jnp.float32)).astype(jnp.bfloat16)
    down_grad = lax.dot_general(
        scaled_hidden, rows_dy, (((0,), (0,)), ((), ())), preferred_element_type=jnp.float32
    ).astype(jnp.bfloat16)
    hidden_grad = prob_rows[:, None] * back_hidden
    grad_gate = (hidden_grad * pre_up * sigmoid_a * (1.0 + pre_gate * (1.0 - sigmoid_a))).astype(jnp.bfloat16)
    grad_up = (hidden_grad * silu_a).astype(jnp.bfloat16)
    return grad_gate, grad_up, score_part, down_grad


def per_device(tokens, grad_out, probs, routes, gate_weight, up_weight, down_weight):
    n_experts = lax.axis_size("expert")
    capacity = min(SLOTS // n_experts, TOK_DEV)
    slots = n_experts * capacity
    tok_rows, width = tokens.shape
    half = width // 2
    top_count = routes.shape[1]
    flat_routes = routes.reshape(-1)
    pair_count = flat_routes.shape[0]
    experts_iota = lax.broadcasted_iota(jnp.int32, (pair_count, n_experts), 1)
    onehot = (flat_routes[:, None] == experts_iota).astype(jnp.int32)
    before = jnp.cumsum(onehot, axis=0) - onehot
    position = jnp.sum(before * onehot, axis=1)
    pair_slot = flat_routes * capacity + position
    slot_iota = lax.broadcasted_iota(jnp.int32, (slots, pair_count), 0)
    placer = (pair_slot[None, :] == slot_iota).astype(jnp.float32)
    token_placer = placer.reshape(slots, tok_rows, top_count).sum(axis=2)
    token_half = token_placer.astype(jnp.bfloat16)
    send_probs = jnp.sum(placer * probs.reshape(1, -1).astype(jnp.float32), axis=1)
    send_probs = jnp.broadcast_to(
        jnp.pad(send_probs.reshape(n_experts, 1, capacity), ((0, 0), (0, 0), (0, 128 - capacity))),
        (n_experts, 8, 128),
    )
    send_x = jnp.dot(token_half, tokens, preferred_element_type=jnp.float32).astype(jnp.bfloat16)
    send_dy = jnp.dot(token_half, grad_out, preferred_element_type=jnp.float32).astype(jnp.bfloat16)
    send = jnp.concatenate(
        [send_x.reshape(n_experts, capacity, width), send_dy.reshape(n_experts, capacity, width)], axis=1
    )
    rows_x, rows_dy, got_probs = dispatch(send, send_probs)
    prob_rows = got_probs[:, 0, :capacity].reshape(slots)
    grad_gate, grad_up, score_part, down_grad = expert_grads(
        rows_x, rows_dy, prob_rows, gate_weight[0], up_weight[0], down_weight[0]
    )
    score_block = jnp.broadcast_to(
        jnp.pad(score_part.reshape(n_experts, 1, capacity), ((0, 0), (0, 0), (0, 128 - capacity))),
        (n_experts, 8, 128),
    )
    back_rows, back_scores = combine(grad_gate, grad_up, score_block, gate_weight[0], up_weight[0])
    back_rows = back_rows.reshape(n_experts, 2, capacity, half)
    token_grad = jnp.einsum(
        "est,ehsw->thw",
        token_half.reshape(n_experts, capacity, tok_rows),
        back_rows,
        preferred_element_type=jnp.float32,
    )
    d_tokens = token_grad.reshape(tok_rows, width).astype(jnp.bfloat16)
    scores = back_scores[:, 0, :capacity].reshape(slots, 1)
    d_probs = jnp.sum(placer * scores, axis=0).reshape(tok_rows, top_count)
    return d_tokens, d_probs, down_grad[None]


def plain_device(tokens, grad_out, probs, routes, gate_weight, up_weight, down_weight):
    n_experts = lax.axis_size("expert")
    capacity = min(SLOTS // n_experts, TOK_DEV)
    slots = n_experts * capacity
    tok_rows = routes.shape[0]
    top_count = routes.shape[1]
    flat_routes = routes.reshape(-1)
    pair_count = flat_routes.shape[0]
    experts_iota = lax.broadcasted_iota(jnp.int32, (pair_count, n_experts), 1)
    onehot = (flat_routes[:, None] == experts_iota).astype(jnp.int32)
    before = jnp.cumsum(onehot, axis=0) - onehot
    position = jnp.sum(before * onehot, axis=1)
    pair_slot = flat_routes * capacity + position
    slot_iota = lax.broadcasted_iota(jnp.int32, (slots, pair_count), 0)
    placer = (pair_slot[None, :] == slot_iota).astype(jnp.float32)
    token_placer = placer.reshape(slots, tok_rows, top_count).sum(axis=2)
    placer_half = placer.astype(jnp.bfloat16)
    token_half = token_placer.astype(jnp.bfloat16)
    send_probs = (
        jnp.dot(placer_half, probs.reshape(-1), preferred_element_type=jnp.float32)
        .astype(jnp.bfloat16)
        .reshape(n_experts, capacity)
    )
    send_x = (
        jnp.dot(token_half, tokens, preferred_element_type=jnp.float32)
        .astype(jnp.bfloat16)
        .reshape(n_experts, capacity, -1)
    )
    send_dy = (
        jnp.dot(token_half, grad_out, preferred_element_type=jnp.float32)
        .astype(jnp.bfloat16)
        .reshape(n_experts, capacity, -1)
    )
    got_x, got_dy, got_probs = (
        lax.all_to_all(send_x, "expert", split_axis=0, concat_axis=0, tiled=True),
        lax.all_to_all(send_dy, "expert", split_axis=0, concat_axis=0, tiled=True),
        lax.all_to_all(send_probs, "expert", split_axis=0, concat_axis=0, tiled=True),
    )
    rows_x, rows_dy = (
        lax.all_gather(got_x, "tensor", axis=2, tiled=True),
        lax.all_gather(got_dy, "tensor", axis=2, tiled=True),
    )
    rows_x = rows_x.reshape(slots, -1)
    rows_dy = rows_dy.reshape(slots, -1)
    prob_rows = got_probs.reshape(slots).astype(jnp.float32)
    w_gate = gate_weight[0]
    w_up = up_weight[0]
    w_down = down_weight[0]
    contract_last = (((1,), (1,)), ((), ()))
    pre_gate = lax.dot_general(rows_x, w_gate, contract_last, preferred_element_type=jnp.float32)
    pre_up = lax.dot_general(rows_x, w_up, contract_last, preferred_element_type=jnp.float32)
    sigmoid_a = jax.nn.sigmoid(pre_gate)
    silu_a = pre_gate * sigmoid_a
    hidden = (silu_a * pre_up).astype(jnp.bfloat16)
    back_hidden = lax.dot_general(
        rows_dy, w_down, contract_last, preferred_element_type=jnp.float32
    )
    score_part = jnp.sum(hidden.astype(jnp.float32) * back_hidden, axis=1)
    scaled_hidden = (prob_rows[:, None] * hidden.astype(jnp.float32)).astype(jnp.bfloat16)
    down_grad = lax.dot_general(
        scaled_hidden, rows_dy, (((0,), (0,)), ((), ())), preferred_element_type=jnp.float32
    ).astype(jnp.bfloat16)
    hidden_grad = prob_rows[:, None] * back_hidden
    grad_gate = (hidden_grad * pre_up * sigmoid_a * (1.0 + pre_gate * (1.0 - sigmoid_a))).astype(
        jnp.bfloat16
    )
    grad_up = (hidden_grad * silu_a).astype(jnp.bfloat16)
    input_grad = jnp.dot(grad_gate, w_gate, preferred_element_type=jnp.float32) + jnp.dot(
        grad_up, w_up, preferred_element_type=jnp.float32
    )
    scores = lax.psum(score_part, "tensor")
    score_block = scores.reshape(n_experts, capacity)
    grad_block = input_grad.reshape(n_experts, capacity, -1)
    placer_back = token_placer.T
    shares = lax.psum_scatter(grad_block, "tensor", scatter_dimension=2, tiled=True)
    back_rows, back_scores = (
        lax.all_to_all(shares, "expert", split_axis=0, concat_axis=0, tiled=True),
        lax.all_to_all(score_block, "expert", split_axis=0, concat_axis=0, tiled=True),
    )
    token_grad = jnp.dot(placer_back, back_rows.reshape(slots, -1), precision=lax.Precision.HIGHEST)
    d_tokens = token_grad.astype(jnp.bfloat16)
    d_probs = jnp.dot(
        placer.T, back_scores.reshape(slots), precision=lax.Precision.HIGHEST
    ).reshape(tok_rows, top_count)
    return (d_tokens, d_probs, down_grad[None])


def solution(mesh):
    regular = mesh.shape["tensor"] == 4 and mesh.shape["expert"] == 8
    return jax.shard_map(
        per_device if regular else plain_device,
        mesh=mesh,
        in_specs=(
            P("expert", "tensor"),
            P("expert", "tensor"),
            P("expert", None),
            P("expert", None),
            P("expert", "tensor", None),
            P("expert", "tensor", None),
            P("expert", "tensor", None),
        ),
        out_specs=(P("expert", "tensor"), P("expert", None), P("expert", "tensor", None)),
        check_vma=False,
    )
```

profile of v0, /device:TPU:0, one launch (start us, length us, event | category | flops | bytes accessed | tf_op | source)
XLA Modules:
  0.0 98.1 jit_solution(18082566455814861529)
XLA Ops:
  0.6 0.8 copy.37
  1.5 0.1 eq.31
  1.6 0.1 eq.34
  1.7 0.6 reduce-window.6
  2.3 0.2 slice_reduce_fusion
  2.8 0.7 multiply_add_fusion
  3.5 0.8 copy.41
  4.4 0.2 select_reduce_fusion.1
  4.6 0.1 convert_reduce_fusion
  4.8 0.1 copy.40
  4.9 0.3 convolution_convert_fusion.2
  5.2 1.2 %convolution_convert_fusion.1 = bf16[320,768]{1,0:T(8,128)(2,1)S(1)} fusion(bf16[320,64]{0,1:T(8,128)(2,1)S(1)} %convert_reduce_fusion, bf16[64,768]{1,0:T(8,128)(2,1)} %param.8), kind=kOutput, calls=%fused_computation.13 | convolution fusion | flops 31703040 | bytes 630784 | tf_op jit(solution)/shard_map/dot_general | solution.py:337
  6.5 34.5 %shard_map.94 = (bf16[320,3072]{1,0:T(8,128)(2,1)S(1)}, bf16[320,3072]{1,0:T(8,128)(2,1)S(1)}, f32[8,8,128]{2,1,0:T(8,128)S(1)}) custom-call(bf16[8,80,768]{2,1,0:T(8,128)(2,1)S(1)} %pad_maximum_fusion.send_ref, f32[8,8,128]{2,1,0:T(8,128)S(1)} %broadcast_in_dim.19.probs_ref), custom_call_target="tpu_custom_call" | custom-call | bytes 7864320 | tf_op jit(solution)/shard_map/pallas_call | solution.py:125
  41.1 1.3 %copy-done.1 = bf16[320,3072]{1,0:T(8,128)(2,1)} copy-done((bf16[320,3072]{1,0:T(8,128)(2,1)}, bf16[320,3072]{1,0:T(8,128)(2,1)S(1)}, u32[]{:S(2)}) %copy-start.1) | copy-done | bytes 1966104
  42.4 7.3 %fusion.12 = f32[320,1344]{1,0:T(8,128)S(1)} fusion(bf16[320,3072]{1,0:T(8,128)(2,1)} %copy-done.1, bf16[1,1344,3072]{2,1,0:T(8,128)(2,1)} %param.11), kind=kOutput, calls=%fused_computation.37 | convolution fusion | flops 2642411520 | bytes 11943936 | tf_op jit(solution)/shard_map/dot_general | solution.py:296
  49.8 5.8 %fusion.14 = f32[320,1344]{1,0:T(8,128)S(1)} fusion(bf16[320,3072]{1,0:T(8,128)(2,1)S(1)} %copy-done.2, bf16[1,1344,3072]{2,1,0:T(8,128)(2,1)} %param.12), kind=kOutput, calls=%fused_computation.39 | convolution fusion | flops 2642411520 | bytes 11943936 | tf_op jit(solution)/shard_map/dot_general | solution.py:297
  55.6 5.3 %fusion.3 = (f32[320]{0:T(512)S(1)}, bf16[320,1344]{1,0:T(8,128)(2,1)}, bf16[320,1344]{1,0:T(8,128)(2,1)S(1)}, bf16[320,1344]{1,0:T(8,128)(2,1)}) fusion(f32[320,1344]{1,0:T(8,128)S(1)} %fusion.14, f32[320,1344]{1,0:T(8,128)S(1)} %fusion.12, f32[320]{0:T(512)S(1)} %mul.83, bf16[320,3072]{1,0:T(8,128)(2,1)S(1)} %get-tuple-element.9, ...), kind=kOutput, calls=%fused_computation.6 | convolution fusion | flops 2650582784 | bytes 16247296 | tf_op jit(solution)/shard_map/dot_general | solution.py:301
  61.0 1.2 %copy-done.3 = bf16[320,1344]{1,0:T(8,128)(2,1)S(1)} copy-done((bf16[320,1344]{1,0:T(8,128)(2,1)S(1)}, bf16[320,1344]{1,0:T(8,128)(2,1)}, u32[]{:S(2)}) %copy-start.3) | copy-done | bytes 860184
  62.2 25.9 %shard_map.95 = (bf16[8,80,384]{2,1,0:T(8,128)(2,1)S(1)}, f32[8,8,128]{2,1,0:T(8,128)S(1)}) custom-call(bf16[320,1344]{1,0:T(8,128)(2,1)S(1)} %get-tuple-element.27.gate_ref, bf16[320,1344]{1,0:T(8,128)(2,1)S(1)} %copy-done.3, f32[8,8,128]{2,1,0:T(8,128)S(1)} %broadcast_in_dim.21.score_ref, bf16[1344,3072]{1,0:T(8,128)(2,1)} %bitcast.55, ...), custom_call_target="tpu_custom_call" | custom-call | flops 5284823040 | bytes 16515072 | tf_op jit(solution)/shard_map/pallas_call | solution.py:260
  88.2 0.9 fusion.6
  89.2 0.1 select_reduce_fusion
  89.3 0.1 reshape.85
  89.4 0.7 copy.43
  90.1 8.1 %fusion = bf16[1,1344,3072]{2,1,0:T(8,128)(2,1)} fusion(bf16[320,3072]{1,0:T(8,128)(2,1)S(1)} %get-tuple-element.9, bf16[320,1344]{1,0:T(8,128)(2,1)} %get-tuple-element.26, f32[320]{0:T(512)S(1)} %mul.83), kind=kOutput, calls=%fused_computation.1 | convolution fusion | flops 2647830528 | bytes 11085056 | tf_op jit(solution)/shard_map/dot_general | solution.py:304
  (31 shorter events, 0.9 us)
Async XLA Ops:
  0.6 4.3 %copy-start = (bf16[64,768]{1,0:T(8,128)(2,1)S(1)}, bf16[64,768]{1,0:T(8,128)(2,1)}, u32[]{:S(2)}) copy-start(bf16[64,768]{1,0:T(8,128)(2,1)} %param.7) | copy-start | bytes 294916
  41.0 1.3 %copy-start.1 = (bf16[320,3072]{1,0:T(8,128)(2,1)}, bf16[320,3072]{1,0:T(8,128)(2,1)S(1)}, u32[]{:S(2)}) copy-start(bf16[320,3072]{1,0:T(8,128)(2,1)S(1)} %get-tuple-element.10) | copy-start | bytes 5898244
  42.4 7.3 %copy-start.2 = (bf16[320,3072]{1,0:T(8,128)(2,1)S(1)}, bf16[320,3072]{1,0:T(8,128)(2,1)}, u32[]{:S(2)}) copy-start(bf16[320,3072]{1,0:T(8,128)(2,1)} %copy-done.1) | copy-start | bytes 5898244
  42.4 13.2 %slice-start = ((s8[8257536]{0:T(1024)(128)(4,1)}), s8[4194304]{0:T(1024)(128)(4,1)S(1)}, s32[]{:S(2)}) async-start(s8[8257536]{0:T(1024)(128)(4,1)} %bitcast.52), calls=%async_computation | async-start | bytes 8388608
  49.8 5.8 %slice-start.1 = ((s8[8257536]{0:T(1024)(128)(4,1)}), s8[4063232]{0:T(1024)(128)(4,1)S(1)}, s32[]{:S(2)}) async-start(s8[8257536]{0:T(1024)(128)(4,1)} %bitcast.52), calls=%async_computation.1 | async-start | bytes 8126464
  61.0 1.2 %copy-start.3 = (bf16[320,1344]{1,0:T(8,128)(2,1)S(1)}, bf16[320,1344]{1,0:T(8,128)(2,1)}, u32[]{:S(2)}) copy-start(bf16[320,1344]{1,0:T(8,128)(2,1)} %get-tuple-element.28.up_ref) | copy-start | bytes 2580484
where the time goes:
time: 98.4 us; the launch traced here: 98.1 us
  Pallas kernels  60.5 us (61%)
  matrix products  28.9 us (29%)
  local copies, waits for them, and re-layouts  6.06 us (6%)
  other arithmetic  1.88 us (2%)
    pallas_call x1, Pallas kernels, dispatch(): pl.pallas_call(functools.partial(dispatch_kernel, n), out_shape=(jax.Shap...  34.5 us
    pallas_call x1, Pallas kernels, combine(): pl.pallas_call(functools.partial(combine_kernel, n), out_shape=(jax.Shape...  25.9 us
    dot_general x1, matrix products, expert_grads(): lax.dot_general(scaled_hidden, rows_dy, (((0,), (0,)), ((), ())), preferr...  8.07 us
    dot_general x1, matrix products, expert_grads(): lax.dot_general(rows_x, w_gate, contract_last, preferred_element_type=jnp...  7.32 us
    dot_general x1, matrix products, expert_grads(): lax.dot_general(rows_x, w_up, contract_last, preferred_element_type=jnp.f...  5.79 us
    dot_general x1, matrix products, expert_grads(): lax.dot_general(rows_dy, w_down, contract_last, preferred_element_type=jn...  5.28 us
    unnamed x14, local copies, waits for them, and re-layouts  3.92 us

commit v1 on v0

--- a/solution.py
+++ b/solution.py
@@ -45,8 +45,8 @@
 
 
 def dispatch_kernel(
-    n, send_ref, probs_ref, x_ref, dy_ref, got_probs_ref,
-    rows, own_sem, out_send, out_recv, core_send, core_recv,
+    n, send_ref, probs_ref, w_gate, w_up, w_down, xy_ref, scaled_ref, gate_ref, up_ref, score_ref,
+    rows, weights, acc, got_probs_ref, prob_rows, load_sem, own_sem, out_send, out_recv, core_send, core_recv,
     side_send, side_recv, pass_send, pass_recv, prob_send, prob_recv,
 ):
     e = lax.axis_index("expert")
@@ -76,6 +76,11 @@
         copy.start()
     for copy in small:
         copy.start()
+    loads = [
+        pltpu.make_async_copy(weight, weights.at[m], load_sem.at[m]) for m, weight in enumerate((w_gate, w_up, w_down))
+    ]
+    for copy in loads:
+        copy.start()
 
     def block(j, index):
         return rows.at[others[j], :, columns(index)]
@@ -83,64 +88,136 @@
     to_core = [remote(block(j, t), block(j, t), core_send.at[j], core_recv.at[j], (e, core)) for j in range(n)]
     to_side = [remote(block(j, t), block(j, t), side_send.at[j], side_recv.at[j], (e, side)) for j in range(n)]
     passed = [remote(block(j, side), block(j, side), pass_send.at[j], pass_recv.at[j], (e, core)) for j in range(n)]
-    lag = 2
-    for j in range(n + lag):
-        if j < n:
-            if j == 0:
-                own.wait()
-            else:
-                remote(send_ref.at[others[j]], block(j, t), out_send.at[j], out_recv.at[j], (others[j], t)).wait_recv()
-            to_side[j].start()
-            to_core[j].start()
-        if j >= lag:
-            k = j - lag
-            remote(block(k, side), block(k, side), side_send.at[k], side_recv.at[k], (e, side)).wait_recv()
-            passed[k].start()
+    for j in range(n):
+        if j == 0:
+            own.wait()
+        else:
+            remote(send_ref.at[others[j]], block(j, t), out_send.at[j], out_recv.at[j], (others[j], t)).wait_recv()
+        to_side[j].start()
+        to_core[j].start()
+    slots, full = xy_ref.shape[1:]
+    hidden = gate_ref.shape[1]
+    reach = 2 * width
+    near = t // 2
+
+    def half_columns(index):
+        return pl.ds(pl.multiple_of(index * reach, 128), reach)
+
+    def assemble(index):
+        for c in range(2):
+            cols = pl.ds(pl.multiple_of(index * reach + c * width, 128), width)
+
+            for k in range(n // 2):
+                first = rows[2 * k, :, cols].astype(jnp.float32)
+                second = rows[2 * k + 1, :, cols].astype(jnp.float32)
+                span = slice(2 * k * cap, 2 * (k + 1) * cap)
+                xy_ref[0, span, cols] = jnp.concatenate([first[:cap], second[:cap]], axis=0).astype(jnp.bfloat16)
+                xy_ref[1, span, cols] = jnp.concatenate([first[cap:], second[cap:]], axis=0).astype(jnp.bfloat16)
+
+    def multiply(m, index, fresh):
+        cols = half_columns(index)
+        for low in range(0, hidden, 512):
+            tile = slice(low, min(low + 512, hidden))
+            part = lax.dot_general(
+                xy_ref[m // 2, :, cols],
+                weights[m, tile, cols],
+                (((1,), (1,)), ((), ())),
+                preferred_element_type=jnp.float32,
+            )
+            acc[m, :, tile] = part if fresh else acc[m, :, tile] + part
+
+    def pass_on(k):
+        remote(block(k, side), block(k, side), side_send.at[k], side_recv.at[k], (e, side)).wait_recv()
+        passed[k].start()
+
+    for k in range(n // 2):
+        pass_on(k)
+    for j in range(n):
+        remote(block(j, core), block(j, core), core_send.at[j], core_recv.at[j], (e, core)).wait_recv()
+    assemble(near)
+    for m in range(3):
+        loads[m].wait()
+        multiply(m, near, True)
+        if m < 2:
+            pass_on(n // 2 + m)
+    for k in range(n // 2 + 2, n):
+        pass_on(k)
     own_probs.wait()
     for j in range(1, n):
         remote(
             probs_ref.at[others[j]], got_probs_ref.at[others[j]], prob_send.at[j], prob_recv.at[j], (others[j], t)
         ).wait_recv()
+    for s in range(n):
+        prob_rows[s * cap : (s + 1) * cap, :] = got_probs_ref[s]
     for j in range(n):
-        remote(block(j, core), block(j, core), core_send.at[j], core_recv.at[j], (e, core)).wait_recv()
         remote(block(j, far), block(j, far), pass_send.at[j], pass_recv.at[j], (e, core)).wait_recv()
-    for k in range(n // 2):
-        for q in range(x_ref.shape[1] // width):
-            cols = slice(q * width, (q + 1) * width)
-            first = rows[2 * k, :, cols].astype(jnp.float32)
-            second = rows[2 * k + 1, :, cols].astype(jnp.float32)
-            span = slice(2 * k * cap, 2 * (k + 1) * cap)
-            x_ref[span, cols] = jnp.concatenate([first[:cap], second[:cap]], axis=0).astype(jnp.bfloat16)
-            dy_ref[span, cols] = jnp.concatenate([first[cap:], second[cap:]], axis=0).astype(jnp.bfloat16)
+    assemble(1 - near)
+    for m in range(3):
+        multiply(m, 1 - near, False)
+
+    @pl.loop(0, slots // 16)
+    def _(r):
+        span = pl.ds(pl.multiple_of(r * 16, 16), 16)
+        prob = prob_rows[span, 0:1]
+        score = jnp.zeros((16, 1), jnp.float32)
+        for low in range(0, hidden, 384):
+            tile = slice(low, min(low + 384, hidden))
+            pre_gate = acc[0, span, tile]
+            pre_up = acc[1, span, tile]
+            back = acc[2, span, tile]
+            sigmoid = jax.nn.sigmoid(pre_gate)
+            silu = pre_gate * sigmoid
+            hid = (silu * pre_up).astype(jnp.bfloat16).astype(jnp.float32)
+            score = score + jnp.sum(hid * back, axis=1, keepdims=True)
+            scaled_ref[span, tile] = (prob * hid).astype(jnp.bfloat16)
+            grad = prob * back
+            gate_ref[span, tile] = (grad * pre_up * sigmoid * (1.0 + pre_gate * (1.0 - sigmoid))).astype(jnp.bfloat16)
+            up_ref[span, tile] = (grad * silu).astype(jnp.bfloat16)
+        score_ref[span, :] = jnp.broadcast_to(score, (16, 128))
+
     for copy in mine + small + to_core + to_side + passed:
         copy.wait_send()
 
 
-def dispatch(send, probs):
+def dispatch(send, probs, w_gate, w_up, w_down):
     n, double, width = send.shape
-    tensor = lax.axis_size("tensor")
-    slots = n * double // 2
-    full = width * tensor
+    cap = double // 2
+    slots = n * cap
+    hidden, full = w_gate.shape
     dma = pltpu.SemaphoreType.DMA
+    small = jax.ShapeDtypeStruct((slots, hidden), jnp.bfloat16)
     return pl.pallas_call(
         functools.partial(dispatch_kernel, n),
         out_shape=(
-            jax.ShapeDtypeStruct((slots, full), jnp.bfloat16),
-            jax.ShapeDtypeStruct((slots, full), jnp.bfloat16),
-            jax.ShapeDtypeStruct(probs.shape, jnp.float32),
-        ),
-        in_specs=[pl.BlockSpec(memory_space=VMEM)] * 2,
-        out_specs=[pl.BlockSpec(memory_space=VMEM)] * 3,
-        scratch_shapes=[pltpu.VMEM((n, double, full), jnp.bfloat16), dma((2,))] + [dma((n,))] * 10,
+            jax.ShapeDtypeStruct((2, slots, full), jnp.bfloat16),
+            small,
+            small,
+            small,
+            jax.ShapeDtypeStruct((slots, 128), jnp.float32),
+        ),
+        in_specs=[pl.BlockSpec(memory_space=VMEM)] * 2 + [pl.BlockSpec(memory_space=pl.ANY)] * 3,
+        out_specs=[pl.BlockSpec(memory_space=VMEM)] * 5,
+        scratch_shapes=[
+            pltpu.VMEM((n, double, full), jnp.bfloat16),
+            pltpu.VMEM((3, hidden, full), jnp.bfloat16),
+            pltpu.VMEM((3, slots, hidden), jnp.float32),
+            pltpu.VMEM((n, cap, 128), jnp.float32),
+            pltpu.VMEM((slots, 128), jnp.float32),
+            dma((3,)),
+            dma((2,)),
+        ]
+        + [dma((n,))] * 10,
         compiler_params=pltpu.CompilerParams(
-            collective_id=0, has_side_effects=True, vmem_limit_bytes=40 * 1024 * 1024
-        ),
-        cost_estimate=pl.CostEstimate(flops=0, bytes_accessed=slots * full * 8, transcendentals=0),
-    )(send, probs)
+            collective_id=0, has_side_effects=True, vmem_limit_bytes=54 * 1024 * 1024
+        ),
+        cost_estimate=pl.CostEstimate(
+            flops=6 * slots * full * hidden, bytes_accessed=6 * hidden * full, transcendentals=slots * hidden
+        ),
+    )(send, probs, w_gate, w_up, w_down)
 
 
 def combine_kernel(
-    n, gate_ref, up_ref, score_ref, w_gate, w_up, got_ref, got_score_ref,
+    n, gate_ref, up_ref, scaled_ref, xy_ref, score_ref, w_gate, w_up, got_ref, got_score_ref, down_ref,
     weights, keep, ship, from_core, mid, from_side, out, score_parts, score_sum,
     load_sem, core_send, core_recv, side_send, side_recv, out_send, out_recv, own_sem,
     sum_send, sum_recv, score_send, score_recv,
@@ -183,6 +260,13 @@
     def span(k):
         return pl.ds(pl.multiple_of(k * chunk, chunk), chunk)
 
+    def down_tile(low):
+        cols = slice(low, low + 256)
+        down_ref[:, cols] = lax.dot_general(
+            scaled_ref[...], xy_ref[1, :, cols], (((0,), (0,)), ((), ())), preferred_element_type=jnp.float32
+        ).astype(jnp.bfloat16)
+
+    down_lows = list(range(0, down_ref.shape[1], 256))
     turns = (2, 3, 1, 0)
     pairs = [flip_all(e // 2, j) for j in range(chunks)]
 
@@ -221,6 +305,7 @@
     product(3, keep.at[1])
     own = pltpu.make_async_copy(out.at[0], got_ref.at[e], own_sem.at[0])
     for j in turns:
+        down_tile(down_lows.pop())
         give_core[j].wait_recv()
         to_side[j].wait_recv()
         total = (
@@ -238,6 +323,8 @@
                 copy = remote(out.at[i], got_ref.at[e], out_send.at[i], out_recv.at[i], (others[i], t))
                 copy.start()
                 sent.append(copy)
+    for low in down_lows:
+        down_tile(low)
     own.wait()
     own_score.wait()
     for j in range(1, n):
@@ -249,7 +336,7 @@
         copy.wait_send()
 
 
-def combine(grad_gate, grad_up, scores, w_gate, w_up):
+def combine(grad_gate, grad_up, scaled, xy, scores, w_gate, w_up):
     tensor = lax.axis_size("tensor")
     slots, hidden = grad_gate.shape
     width = w_gate.shape[1] // tensor
@@ -262,9 +349,10 @@
         out_shape=(
             jax.ShapeDtypeStruct((n, chunk, width // 2), jnp.bfloat16),
             jax.ShapeDtypeStruct(scores.shape, jnp.float32),
-        ),
-        in_specs=[pl.BlockSpec(memory_space=VMEM)] * 3 + [pl.BlockSpec(memory_space=pl.ANY)] * 2,
-        out_specs=[pl.BlockSpec(memory_space=VMEM)] * 2,
+            jax.ShapeDtypeStruct(w_gate.shape, jnp.bfloat16),
+        ),
+        in_specs=[pl.BlockSpec(memory_space=VMEM)] * 5 + [pl.BlockSpec(memory_space=pl.ANY)] * 2,
+        out_specs=[pl.BlockSpec(memory_space=VMEM)] * 3,
         scratch_shapes=[
             pltpu.VMEM((tensor, 2, hidden, width), jnp.bfloat16),
             pltpu.VMEM((2, slots, width), jnp.float32),
@@ -283,31 +371,12 @@
             dma((n,)), dma((n,)),
         ],
         compiler_params=pltpu.CompilerParams(
-            collective_id=1, has_side_effects=True, vmem_limit_bytes=50 * 1024 * 1024
+            collective_id=1, has_side_effects=True, vmem_limit_bytes=54 * 1024 * 1024
         ),
         cost_estimate=pl.CostEstimate(
             flops=4 * slots * hidden * width * tensor, bytes_accessed=4 * hidden * width * tensor, transcendentals=0
         ),
-    )(grad_gate, grad_up, scores, w_gate, w_up)
-
-
-def expert_grads(rows_x, rows_dy, prob_rows, w_gate, w_up, w_down):
-    contract_last = (((1,), (1,)), ((), ()))
-    pre_gate = lax.dot_general(rows_x, w_gate, contract_last, preferred_element_type=jnp.float32)
-    pre_up = lax.dot_general(rows_x, w_up, contract_last, preferred_element_type=jnp.float32)
-    sigmoid_a = jax.nn.sigmoid(pre_gate)
-    silu_a = pre_gate * sigmoid_a
-    hidden = (silu_a * pre_up).astype(jnp.bfloat16)
-    back_hidden = lax.dot_general(rows_dy, w_down, contract_last, preferred_element_type=jnp.float32)
-    score_part = jnp.sum(hidden.astype(jnp.float32) * back_hidden, axis=1)
-    scaled_hidden = (prob_rows[:, None] * hidden.astype(jnp.float32)).astype(jnp.bfloat16)
-    down_grad = lax.dot_general(
-        scaled_hidden, rows_dy, (((0,), (0,)), ((), ())), preferred_element_type=jnp.float32
-    ).astype(jnp.bfloat16)
-    hidden_grad = prob_rows[:, None] * back_hidden
-    grad_gate = (hidden_grad * pre_up * sigmoid_a * (1.0 + pre_gate * (1.0 - sigmoid_a))).astype(jnp.bfloat16)
-    grad_up = (hidden_grad * silu_a).astype(jnp.bfloat16)
-    return grad_gate, grad_up, score_part, down_grad
+    )(grad_gate, grad_up, scaled, xy, scores, w_gate, w_up)
 
 
 def per_device(tokens, grad_out, probs, routes, gate_weight, up_weight, down_weight):
@@ -329,25 +398,23 @@
     token_placer = placer.reshape(slots, tok_rows, top_count).sum(axis=2)
     token_half = token_placer.astype(jnp.bfloat16)
     send_probs = jnp.sum(placer * probs.reshape(1, -1).astype(jnp.float32), axis=1)
-    send_probs = jnp.broadcast_to(
-        jnp.pad(send_probs.reshape(n_experts, 1, capacity), ((0, 0), (0, 0), (0, 128 - capacity))),
-        (n_experts, 8, 128),
-    )
+    send_probs = jnp.broadcast_to(send_probs.reshape(n_experts, capacity, 1), (n_experts, capacity, 128))
     send_x = jnp.dot(token_half, tokens, preferred_element_type=jnp.float32).astype(jnp.bfloat16)
     send_dy = jnp.dot(token_half, grad_out, preferred_element_type=jnp.float32).astype(jnp.bfloat16)
     send = jnp.concatenate(
         [send_x.reshape(n_experts, capacity, width), send_dy.reshape(n_experts, capacity, width)], axis=1
     )
-    rows_x, rows_dy, got_probs = dispatch(send, send_probs)
-    prob_rows = got_probs[:, 0, :capacity].reshape(slots)
-    grad_gate, grad_up, score_part, down_grad = expert_grads(
-        rows_x, rows_dy, prob_rows, gate_weight[0], up_weight[0], down_weight[0]
-    )
+    xy, scaled, grad_gate, grad_up, score_part = dispatch(
+        send, send_probs, gate_weight[0], up_weight[0], down_weight[0]
+    )
+    score_part = score_part[:, 0]
     score_block = jnp.broadcast_to(
         jnp.pad(score_part.reshape(n_experts, 1, capacity), ((0, 0), (0, 0), (0, 128 - capacity))),
         (n_experts, 8, 128),
     )
-    back_rows, back_scores = combine(grad_gate, grad_up, score_block, gate_weight[0], up_weight[0])
+    back_rows, back_scores, down_grad = combine(
+        grad_gate, grad_up, scaled, xy, score_block, gate_weight[0], up_weight[0]
+    )
     back_rows = back_rows.reshape(n_experts, 2, capacity, half)
     token_grad = jnp.einsum(
         "est,ehsw->thw",

time: 98.4 us -> 103 us (1.047)
  matrix products: 28.9 us -> 2.39 us
  Pallas kernels: 60.5 us -> 81.7 us
  local copies, waits for them, and re-layouts: 6.06 us -> 15.1 us
    dot_general x4 -> x0, matrix products: 26.5 us -> none  [the longest x1 8.07 us: expert_grads(): lax.dot_general(scaled_hidden, rows_dy, (((0,), (0,)), ((), ())), preferr...]
    pallas_call x1, Pallas kernels: 34.5 us -> 45.4 us  [dispatch(): pl.pallas_call(functools.partial(dispatch_kernel, n), out_shape=(jax.Shap...]
    pallas_call x1, Pallas kernels: 25.9 us -> 36.3 us  [combine(): pl.pallas_call(functools.partial(combine_kernel, n), out_shape=(jax.Shape...]
    unnamed x14 -> x5, local copies, waits for them, and re-layouts: 3.92 us -> 8.86 us
    slice x2, local copies, waits for them, and re-layouts: 0.23 us -> 1.27 us  [the longest x1 1.06 us: per_device(): score_part = score_part[:, 0]]
where the time goes in v1:
time: 103 us
  Pallas kernels  81.7 us (79%)
  local copies, waits for them, and re-layouts  15.1 us (15%)
  other arithmetic  2.83 us (3%)
  matrix products  2.39 us (2%)
    pallas_call x1, Pallas kernels, dispatch(): pl.pallas_call(functools.partial(dispatch_kernel, n), out_shape=(jax.Shap...  45.4 us
    pallas_call x1, Pallas kernels, combine(): pl.pallas_call(functools.partial(combine_kernel, n), out_shape=(jax.Shape...  36.3 us
    unnamed x5, local copies, waits for them, and re-layouts  8.86 us

profile of v1, /device:TPU:0, one launch (start us, length us, event | category | flops | bytes accessed | tf_op | source)
XLA Modules:
  0.0 102.7 jit_solution(8817496888835342332)
XLA Ops:
  0.6 0.8 copy.37
  1.6 0.1 eq.34
  1.7 0.6 reduce-window.6
  2.3 0.2 slice_reduce_fusion.1
  2.8 0.7 multiply_add_fusion
  3.5 0.8 copy.41
  4.4 0.2 select_reduce_fusion.1
  4.6 0.1 convert_reduce_fusion
  4.7 0.1 copy.40
  4.9 0.8 broadcast_in_dim.19.probs_ref
  5.6 0.3 convolution_convert_fusion.1
  5.9 1.2 %convolution_convert_fusion = bf16[320,768]{1,0:T(8,128)(2,1)S(1)} fusion(bf16[320,64]{0,1:T(8,128)(2,1)S(1)} %convert_reduce_fusion, bf16[64,768]{1,0:T(8,128)(2,1)} %param.8), kind=kOutput, calls=%fused_computation | convolution fusion | flops 31703040 | bytes 630784 | tf_op jit(solution)/shard_map/dot_general | solution.py:403
  7.2 1.0 pad_maximum_fusion.send_ref
  8.2 45.4 %shard_map.94 = (bf16[2,320,3072]{2,1,0:T(8,128)(2,1)}, bf16[320,1344]{1,0:T(8,128)(2,1)}, bf16[320,1344]{1,0:T(8,128)(2,1)}, bf16[320,1344]{1,0:T(8,128)(2,1)}, f32[320,128]{1,0:T(8,128)}) custom-call(bf16[8,80,768]{2,1,0:T(8,128)(2,1)} %pad_maximum_fusion.send_ref, f32[8,40,128]{2,1,0:T(8,128)} %broadcast_in_dim.19.probs_ref, bf16[1344,3072]{1,0:T(8,128)(2,1)} %bitcast.32, ...), custom_call_target="tpu_custom_call" | custom-call | flops 7927234560 | bytes 24772608 | tf_op jit(solution)/shard_map/pallas_call | solution.py:189
  53.5 1.1 %slice_reduce_fusion = f32[320]{0:T(512)S(1)} fusion(f32[320,128]{1,0:T(8,128)} %get-tuple-element.15), kind=kLoop, calls=%fused_computation.10 | loop fusion | bytes 2560 | tf_op jit(solution)/shard_map/slice | solution.py:410
  54.7 0.6 broadcast_in_dim.21.score_ref
  55.3 36.3 %shard_map.95 = (bf16[8,80,384]{2,1,0:T(8,128)(2,1)}, f32[8,8,128]{2,1,0:T(8,128)}, bf16[1344,3072]{1,0:T(8,128)(2,1)}) custom-call(bf16[320,1344]{1,0:T(8,128)(2,1)} %get-tuple-element.11.gate_ref, bf16[320,1344]{1,0:T(8,128)(2,1)} %get-tuple-element.12.up_ref, bf16[320,1344]{1,0:T(8,128)(2,1)} %get-tuple-element.13.scaled_ref, ...), custom_call_target="tpu_custom_call" | custom-call | flops 5284823040 | bytes 16515072 | tf_op jit(solution)/shard_map/pallas_call | solution.py:347
  91.6 1.1 %copy.44 = bf16[8,2,5,8,384]{4,3,1,2,0:T(8,128)(2,1)S(1)} copy(bf16[8,2,5,8,384]{4,3,2,1,0:T(8,128)(2,1)} %bitcast.40) | data formatting | bytes 983040 | tf_op jit(solution)/shard_map/est,ehsw->thw/dot_general | solution.py:419
  92.7 0.9 fusion
  93.6 0.8 slice_reduce_fusion.2
  94.5 0.1 select_reduce_fusion
  94.6 0.1 reshape.78
  94.7 0.7 copy.43
  95.4 7.4 %copy.46 = bf16[1,1344,3072]{2,1,0:T(8,128)(2,1)} copy(bf16[1,1344,3072]{2,1,0:T(8,128)(2,1)} %bitcast.36) | data formatting | bytes 16515072
  (15 shorter events, 0.8 us)
Async XLA Ops:
  0.6 5.0 %copy-start = (bf16[64,768]{1,0:T(8,128)(2,1)S(1)}, bf16[64,768]{1,0:T(8,128)(2,1)}, u32[]{:S(2)}) copy-start(bf16[64,768]{1,0:T(8,128)(2,1)} %param.7) | copy-start | bytes 294916

commit v2 on v1

--- a/solution.py
+++ b/solution.py
@@ -45,8 +45,8 @@
 
 
 def dispatch_kernel(
-    n, send_ref, probs_ref, w_gate, w_up, w_down, xy_ref, scaled_ref, gate_ref, up_ref, score_ref,
-    rows, weights, acc, got_probs_ref, prob_rows, load_sem, own_sem, out_send, out_recv, core_send, core_recv,
+    n, send_ref, probs_ref, w_gate, w_up, w_down, dy_ref, scaled_ref, gate_ref, up_ref, score_ref,
+    rows, weights, acc, x_rows, score_rows, got_probs_ref, prob_rows, load_sem, own_sem, out_send, out_recv, core_send, core_recv,
     side_send, side_recv, pass_send, pass_recv, prob_send, prob_recv,
 ):
     e = lax.axis_index("expert")
@@ -95,7 +95,7 @@
             remote(send_ref.at[others[j]], block(j, t), out_send.at[j], out_recv.at[j], (others[j], t)).wait_recv()
         to_side[j].start()
         to_core[j].start()
-    slots, full = xy_ref.shape[1:]
+    slots = dy_ref.shape[0]
     hidden = gate_ref.shape[1]
     reach = 2 * width
     near = t // 2
@@ -111,15 +111,15 @@
                 first = rows[2 * k, :, cols].astype(jnp.float32)
                 second = rows[2 * k + 1, :, cols].astype(jnp.float32)
                 span = slice(2 * k * cap, 2 * (k + 1) * cap)
-                xy_ref[0, span, cols] = jnp.concatenate([first[:cap], second[:cap]], axis=0).astype(jnp.bfloat16)
-                xy_ref[1, span, cols] = jnp.concatenate([first[cap:], second[cap:]], axis=0).astype(jnp.bfloat16)
+                x_rows[span, cols] = jnp.concatenate([first[:cap], second[:cap]], axis=0).astype(jnp.bfloat16)
+                dy_ref[span, cols] = jnp.concatenate([first[cap:], second[cap:]], axis=0).astype(jnp.bfloat16)
 
     def multiply(m, index, fresh):
         cols = half_columns(index)
         for low in range(0, hidden, 512):
             tile = slice(low, min(low + 512, hidden))
             part = lax.dot_general(
-                xy_ref[m // 2, :, cols],
+                (dy_ref if m == 2 else x_rows)[:, cols],
                 weights[m, tile, cols],
                 (((1,), (1,)), ((), ())),
                 preferred_element_type=jnp.float32,
@@ -173,7 +173,12 @@
             grad = prob * back
             gate_ref[span, tile] = (grad * pre_up * sigmoid * (1.0 + pre_gate * (1.0 - sigmoid))).astype(jnp.bfloat16)
             up_ref[span, tile] = (grad * silu).astype(jnp.bfloat16)
-        score_ref[span, :] = jnp.broadcast_to(score, (16, 128))
+        score_rows[span, :] = jnp.broadcast_to(score, (16, 128))
+
+    diagonal = lax.broadcasted_iota(jnp.int32, (cap, 128), 0) == lax.broadcasted_iota(jnp.int32, (cap, 128), 1)
+    for s in range(n):
+        line = jnp.sum(jnp.where(diagonal, score_rows[s * cap : (s + 1) * cap, :], 0.0), axis=0, keepdims=True)
+        score_ref[s] = jnp.broadcast_to(line, score_ref.shape[1:])
 
     for copy in mine + small + to_core + to_side + passed:
         copy.wait_send()
@@ -189,11 +194,11 @@
     return pl.pallas_call(
         functools.partial(dispatch_kernel, n),
         out_shape=(
-            jax.ShapeDtypeStruct((2, slots, full), jnp.bfloat16),
+            jax.ShapeDtypeStruct((slots, full), jnp.bfloat16),
             small,
             small,
             small,
-            jax.ShapeDtypeStruct((slots, 128), jnp.float32),
+            jax.ShapeDtypeStruct((n, 8, 128), jnp.float32),
         ),
         in_specs=[pl.BlockSpec(memory_space=VMEM)] * 2 + [pl.BlockSpec(memory_space=pl.ANY)] * 3,
         out_specs=[pl.BlockSpec(memory_space=VMEM)] * 5,
@@ -201,6 +206,8 @@
             pltpu.VMEM((n, double, full), jnp.bfloat16),
             pltpu.VMEM((3, hidden, full), jnp.bfloat16),
             pltpu.VMEM((3, slots, hidden), jnp.float32),
+            pltpu.VMEM((slots, full), jnp.bfloat16),
+            pltpu.VMEM((slots, 128), jnp.float32),
             pltpu.VMEM((n, cap, 128), jnp.float32),
             pltpu.VMEM((slots, 128), jnp.float32),
             dma((3,)),
@@ -217,7 +224,7 @@
 
 
 def combine_kernel(
-    n, gate_ref, up_ref, scaled_ref, xy_ref, score_ref, w_gate, w_up, got_ref, got_score_ref, down_ref,
+    n, gate_ref, up_ref, score_ref, w_gate, w_up, got_ref, got_score_ref,
     weights, keep, ship, from_core, mid, from_side, out, score_parts, score_sum,
     load_sem, core_send, core_recv, side_send, side_recv, out_send, out_recv, own_sem,
     sum_send, sum_recv, score_send, score_recv,
@@ -260,13 +267,6 @@
     def span(k):
         return pl.ds(pl.multiple_of(k * chunk, chunk), chunk)
 
-    def down_tile(low):
-        cols = slice(low, low + 256)
-        down_ref[:, cols] = lax.dot_general(
-            scaled_ref[...], xy_ref[1, :, cols], (((0,), (0,)), ((), ())), preferred_element_type=jnp.float32
-        ).astype(jnp.bfloat16)
-
-    down_lows = list(range(0, down_ref.shape[1], 256))
     turns = (2, 3, 1, 0)
     pairs = [flip_all(e // 2, j) for j in range(chunks)]
 
@@ -305,7 +305,6 @@
     product(3, keep.at[1])
     own = pltpu.make_async_copy(out.at[0], got_ref.at[e], own_sem.at[0])
     for j in turns:
-        down_tile(down_lows.pop())
         give_core[j].wait_recv()
         to_side[j].wait_recv()
         total = (
@@ -323,8 +322,6 @@
                 copy = remote(out.at[i], got_ref.at[e], out_send.at[i], out_recv.at[i], (others[i], t))
                 copy.start()
                 sent.append(copy)
-    for low in down_lows:
-        down_tile(low)
     own.wait()
     own_score.wait()
     for j in range(1, n):
@@ -336,7 +333,7 @@
         copy.wait_send()
 
 
-def combine(grad_gate, grad_up, scaled, xy, scores, w_gate, w_up):
+def combine(grad_gate, grad_up, scores, w_gate, w_up):
     tensor = lax.axis_size("tensor")
     slots, hidden = grad_gate.shape
     width = w_gate.shape[1] // tensor
@@ -349,10 +346,9 @@
         out_shape=(
             jax.ShapeDtypeStruct((n, chunk, width // 2), jnp.bfloat16),
             jax.ShapeDtypeStruct(scores.shape, jnp.float32),
-            jax.ShapeDtypeStruct(w_gate.shape, jnp.bfloat16),
-        ),
-        in_specs=[pl.BlockSpec(memory_space=VMEM)] * 5 + [pl.BlockSpec(memory_space=pl.ANY)] * 2,
-        out_specs=[pl.BlockSpec(memory_space=VMEM)] * 3,
+        ),
+        in_specs=[pl.BlockSpec(memory_space=VMEM)] * 3 + [pl.BlockSpec(memory_space=pl.ANY)] * 2,
+        out_specs=[pl.BlockSpec(memory_space=VMEM)] * 2,
         scratch_shapes=[
             pltpu.VMEM((tensor, 2, hidden, width), jnp.bfloat16),
             pltpu.VMEM((2, slots, width), jnp.float32),
@@ -376,7 +372,33 @@
         cost_estimate=pl.CostEstimate(
             flops=4 * slots * hidden * width * tensor, bytes_accessed=4 * hidden * width * tensor, transcendentals=0
         ),
-    )(grad_gate, grad_up, scaled, xy, scores, w_gate, w_up)
+    )(grad_gate, grad_up, scores, w_gate, w_up)
+
+
+def down_kernel(scaled_ref, dy_ref, out_ref, turned):
+    @pl.when(pl.program_id(0) == 0)
+    def _():
+        turned[...] = scaled_ref[...].T
+
+    out_ref[...] = jnp.dot(turned[...], dy_ref[...], preferred_element_type=jnp.float32).astype(jnp.bfloat16)
+
+
+def down_product(scaled, rows_dy):
+    slots, hidden = scaled.shape
+    full = rows_dy.shape[1]
+    tile = 512
+    return pl.pallas_call(
+        down_kernel,
+        grid=(full // tile,),
+        out_shape=jax.ShapeDtypeStruct((hidden, full), jnp.bfloat16),
+        in_specs=[pl.BlockSpec((slots, hidden), lambda c: (0, 0)), pl.BlockSpec((slots, tile), lambda c: (0, c))],
+        out_specs=pl.BlockSpec((hidden, tile), lambda c: (0, c)),
+        scratch_shapes=[pltpu.VMEM((hidden, slots), jnp.bfloat16)],
+        compiler_params=pltpu.CompilerParams(vmem_limit_bytes=24 * 1024 * 1024),
+        cost_estimate=pl.CostEstimate(
+            flops=2 * slots * hidden * full, bytes_accessed=2 * hidden * full, transcendentals=0
+        ),
+    )(scaled, rows_dy)
 
 
 def per_device(tokens, grad_out, probs, routes, gate_weight, up_weight, down_weight):
@@ -386,45 +408,45 @@
     tok_rows, width = tokens.shape
     half = width // 2
     top_count = routes.shape[1]
-    flat_routes = routes.reshape(-1)
-    pair_count = flat_routes.shape[0]
-    experts_iota = lax.broadcasted_iota(jnp.int32, (pair_count, n_experts), 1)
-    onehot = (flat_routes[:, None] == experts_iota).astype(jnp.int32)
-    before = jnp.cumsum(onehot, axis=0) - onehot
-    position = jnp.sum(before * onehot, axis=1)
-    pair_slot = flat_routes * capacity + position
-    slot_iota = lax.broadcasted_iota(jnp.int32, (slots, pair_count), 0)
-    placer = (pair_slot[None, :] == slot_iota).astype(jnp.float32)
-    token_placer = placer.reshape(slots, tok_rows, top_count).sum(axis=2)
-    token_half = token_placer.astype(jnp.bfloat16)
-    send_probs = jnp.sum(placer * probs.reshape(1, -1).astype(jnp.float32), axis=1)
-    send_probs = jnp.broadcast_to(send_probs.reshape(n_experts, capacity, 1), (n_experts, capacity, 128))
-    send_x = jnp.dot(token_half, tokens, preferred_element_type=jnp.float32).astype(jnp.bfloat16)
-    send_dy = jnp.dot(token_half, grad_out, preferred_element_type=jnp.float32).astype(jnp.bfloat16)
-    send = jnp.concatenate(
-        [send_x.reshape(n_experts, capacity, width), send_dy.reshape(n_experts, capacity, width)], axis=1
-    )
-    xy, scaled, grad_gate, grad_up, score_part = dispatch(
+    experts = lax.broadcasted_iota(jnp.int32, (tok_rows, top_count, n_experts), 2)
+    named = (routes[:, :, None] == experts).astype(jnp.float32)
+    earlier = (
+        lax.broadcasted_iota(jnp.int32, (tok_rows, tok_rows), 0)
+        > lax.broadcasted_iota(jnp.int32, (tok_rows, tok_rows), 1)
+    ).astype(jnp.bfloat16)
+    before = jnp.dot(earlier, named.sum(axis=1).astype(jnp.bfloat16), preferred_element_type=jnp.float32)
+    position = jnp.sum(named * before[:, None, :], axis=2).astype(jnp.int32)
+    pair_slot = routes * capacity + position
+    across = pair_slot.T
+    slot_iota = lax.broadcasted_iota(jnp.int32, (slots, tok_rows), 0)
+    probs_across = probs.T.astype(jnp.float32)
+    weighted = sum(
+        jnp.where(across[k][None, :] == slot_iota, probs_across[k][None, :], 0.0) for k in range(top_count)
+    ).astype(jnp.bfloat16)
+    send_probs = jnp.dot(
+        weighted, jnp.ones((tok_rows, 128), jnp.bfloat16), preferred_element_type=jnp.float32
+    ).reshape(n_experts, capacity, 128)
+    code = routes.T * (2 * capacity) + position.T
+    code = jnp.concatenate([code, code + capacity], axis=1)
+    row_iota = lax.broadcasted_iota(jnp.int32, (2 * slots, 2 * tok_rows), 0)
+    placer = sum((code[k][None, :] == row_iota).astype(jnp.float32) for k in range(top_count)).astype(jnp.bfloat16)
+    send = (
+        jnp.dot(placer, jnp.concatenate([tokens, grad_out], axis=0), preferred_element_type=jnp.float32)
+        .astype(jnp.bfloat16)
+        .reshape(n_experts, 2 * capacity, width)
+    )
+    rows_dy, scaled, grad_gate, grad_up, score_block = dispatch(
         send, send_probs, gate_weight[0], up_weight[0], down_weight[0]
     )
-    score_part = score_part[:, 0]
-    score_block = jnp.broadcast_to(
-        jnp.pad(score_part.reshape(n_experts, 1, capacity), ((0, 0), (0, 0), (0, 128 - capacity))),
-        (n_experts, 8, 128),
-    )
-    back_rows, back_scores, down_grad = combine(
-        grad_gate, grad_up, scaled, xy, score_block, gate_weight[0], up_weight[0]
-    )
-    back_rows = back_rows.reshape(n_experts, 2, capacity, half)
-    token_grad = jnp.einsum(
-        "est,ehsw->thw",
-        token_half.reshape(n_experts, capacity, tok_rows),
-        back_rows,
-        preferred_element_type=jnp.float32,
-    )
-    d_tokens = token_grad.reshape(tok_rows, width).astype(jnp.bfloat16)
-    scores = back_scores[:, 0, :capacity].reshape(slots, 1)
-    d_probs = jnp.sum(placer * scores, axis=0).reshape(tok_rows, top_count)
+    back_rows, back_scores = combine(grad_gate, grad_up, score_block, gate_weight[0], up_weight[0])
+    down_grad = down_product(scaled, rows_dy)
+    token_grad = lax.dot_general(
+        placer, back_rows.reshape(2 * slots, half), (((0,), (0,)), ((), ())), preferred_element_type=jnp.float32
+    )
+    d_tokens = jnp.concatenate([token_grad[:tok_rows], token_grad[tok_rows:]], axis=1).astype(jnp.bfloat16)
+    scores = back_scores[:, 0, :capacity].reshape(1, 1, slots)
+    chosen = pair_slot[:, :, None] == lax.broadcasted_iota(jnp.int32, (tok_rows, top_count, slots), 2)
+    d_probs = jnp.sum(jnp.where(chosen, scores, 0.0), axis=2)
     return d_tokens, d_probs, down_grad[None]
 
 

time: 103 us -> 95.4 us (0.926)
  local copies, waits for them, and re-layouts: 15.1 us -> 0.89 us
  matrix products: 2.39 us -> 4.8 us
  other arithmetic: 2.83 us -> 4.96 us
  Pallas kernels: 81.7 us -> 83.6 us
    unnamed x5 -> x4, local copies, waits for them, and re-layouts: 8.86 us -> 0.01 us
    pallas_call x0 -> x1, Pallas kernels: none -> 7.21 us  [down_product(): pl.pallas_call(down_kernel, grid=(full // tile,), out_shape=jax.ShapeDtyp...]
    pallas_call x1, Pallas kernels: 36.3 us -> 31.8 us  [combine(): pl.pallas_call(functools.partial(combine_kernel, n), out_shape=(jax.Shape...]
    dot_general x3 -> x4, matrix products: 2.39 us -> 4.8 us  [the longest x1 2.33 us: per_device(): jnp.dot(placer, jnp.concatenate([tokens, grad_out], axis=0), preferred_el...]
    reduce_sum x4 -> x3, other arithmetic: 0.49 us -> 2.17 us  [the longest x1 0.77 us: per_device(): d_probs = jnp.sum(jnp.where(chosen, scores, 0.0), axis=2)]
    broadcast_in_dim x4 -> x2, local copies, waits for them, and re-layouts: 1.48 us -> 0.09 us  [the longest x1 0.08 us: per_device(): d_probs = jnp.sum(jnp.where(chosen, scores, 0.0), axis=2)]
    slice x3 -> x2, local copies, waits for them, and re-layouts: 2.04 us -> 0.78 us  [the longest x1 0.77 us: per_device(): scores = back_scores[:, 0, :capacity].reshape(1, 1, slots)]
    dot_general x1 -> x0, local copies, waits for them, and re-layouts: 1.08 us -> none  [per_device(): jnp.einsum('est,ehsw->thw', token_half.reshape(n_experts, capacity, tok_r...]
where the time goes in v2:
time: 95.4 us; the launch traced here: 95 us
  Pallas kernels  83.6 us (88%)
  other arithmetic  4.96 us (5%)
  matrix products  4.8 us (5%)
    pallas_call x1, Pallas kernels, dispatch(): pl.pallas_call(functools.partial(dispatch_kernel, n), out_shape=(jax.Shap...  44.6 us
    pallas_call x1, Pallas kernels, combine(): pl.pallas_call(functools.partial(combine_kernel, n), out_shape=(jax.Shape...  31.8 us
    pallas_call x1, Pallas kernels, down_product(): pl.pallas_call(down_kernel, grid=(full // tile,), out_shape=jax.ShapeDtyp...  7.21 us
    dot_general x1, matrix products, per_device(): jnp.dot(placer, jnp.concatenate([tokens, grad_out], axis=0), preferred_el...  2.33 us

profile of v2, /device:TPU:0, one launch (start us, length us, event | category | flops | bytes accessed | tf_op | source)
XLA Modules:
  0.0 95.0 jit_solution(15106033031388188672)
XLA Ops:
  0.6 0.7 convert_bitcast_fusion
  1.3 0.7 convert_reduce_fusion
  2.0 0.1 fusion.14
  2.1 0.7 select_reduce_fusion.1
  2.9 0.7 multiply_add_fusion.1
  3.5 0.7 broadcast_add_fusion
  4.2 0.1 pad_add_fusion
  4.3 1.0 %fusion.3.probs_ref = f32[8,40,128]{2,1,0:T(8,128)} fusion(f32[64]{0:T(128)S(1)} %get-tuple-element.26, s32[64]{0:T(128)S(1)} %get-tuple-element.22, f32[64]{0:T(128)S(1)} %get-tuple-element.27, s32[64]{0:T(128)S(1)} %get-tuple-element.23, f32[64]{0:T(128)S(1)} %get-tuple-element.28, s32[64]{0:T(128)S(1)} %get-tuple-element.24, ...), kind=kOutput, calls=%fused_computation.14 | convolution fusion | flops 5488640 | bytes 167168 | tf_op jit(solution)/shard_map/dot_general | solution.py:426
  5.3 2.3 %convolution_convert_fusion = bf16[640,768]{1,0:T(8,128)(2,1)} fusion(bf16[64,768]{1,0:T(8,128)(2,1)} %param.8, bf16[64,768]{1,0:T(8,128)(2,1)} %param.7, s32[128]{0:T(128)S(1)} %get-tuple-element.30, s32[128]{0:T(128)S(1)} %get-tuple-element.31, s32[128]{0:T(128)S(1)} %get-tuple-element.32, s32[128]{0:T(128)S(1)} %get-tuple-element.29), kind=kOutput, calls=%fused_computation | convolution fusion | flops 127696896 | bytes 1181696 | tf_op jit(solution)/shard_map/dot_general | solution.py:434
  7.6 44.6 %shard_map.94 = (bf16[320,3072]{1,0:T(8,128)(2,1)}, bf16[320,1344]{1,0:T(8,128)(2,1)}, bf16[320,1344]{1,0:T(8,128)(2,1)}, bf16[320,1344]{1,0:T(8,128)(2,1)}, f32[8,8,128]{2,1,0:T(8,128)}) custom-call(bf16[8,80,768]{2,1,0:T(8,128)(2,1)} %bitcast.39, f32[8,40,128]{2,1,0:T(8,128)} %fusion.3.probs_ref, bf16[1344,3072]{1,0:T(8,128)(2,1)} %bitcast.42, ...), custom_call_target="tpu_custom_call" | custom-call | flops 7927234560 | bytes 24772608 | tf_op jit(solution)/shard_map/pallas_call | solution.py:194
  52.3 0.0 copy-start
  52.3 0.0 copy-start.1
  52.3 31.8 %shard_map.95 = (bf16[8,80,384]{2,1,0:T(8,128)(2,1)}, f32[8,8,128]{2,1,0:T(8,128)}) custom-call(bf16[320,1344]{1,0:T(8,128)(2,1)} %get-tuple-element.10.gate_ref, bf16[320,1344]{1,0:T(8,128)(2,1)} %get-tuple-element.11.up_ref, f32[8,8,128]{2,1,0:T(8,128)} %get-tuple-element.12.score_ref, bf16[1344,3072]{1,0:T(8,128)(2,1)} %bitcast.43, ...), custom_call_target="tpu_custom_call" | custom-call | flops 5284823040 | bytes 16515072 | tf_op jit(solution)/shard_map/pallas_call | solution.py:344
  84.1 1.4 %convolution_convert_fusion.1 = bf16[128,384]{1,0:T(8,128)(2,1)S(1)} fusion(bf16[640,384]{1,0:T(8,128)(2,1)} %bitcast.46, s32[128]{0:T(128)S(1)} %get-tuple-element.30, s32[128]{0:T(128)S(1)} %get-tuple-element.31, s32[128]{0:T(128)S(1)} %get-tuple-element.32, s32[128]{0:T(128)S(1)} %get-tuple-element.29), kind=kOutput, calls=%fused_computation.1 | convolution fusion | flops 63946752 | bytes 591872 | tf_op jit(solution)/shard_map/dot_general | solution.py:443
  85.5 0.7 pad_maximum_fusion
  86.2 0.8 slice_reduce_fusion
  86.9 0.1 broadcast_in_dim.71
  87.0 0.8 select_reduce_fusion
  87.8 0.0 copy-done
  87.8 0.0 copy-done.1
  87.8 7.2 %shard_map.96 = bf16[1344,3072]{1,0:T(8,128)(2,1)} custom-call(bf16[320,1344]{1,0:T(8,128)(2,1)S(1)} %copy-done.1, bf16[320,3072]{1,0:T(8,128)(2,1)S(1)} %copy-done), custom_call_target="tpu_custom_call" | custom-call | flops 2642411520 | bytes 8257536 | tf_op jit(solution)/shard_map/pallas_call | solution.py:390
  (5 shorter events, 0.0 us)
Async XLA Ops:
  52.3 35.5 %copy-start = (bf16[320,3072]{1,0:T(8,128)(2,1)S(1)}, bf16[320,3072]{1,0:T(8,128)(2,1)}, u32[]{:S(2)}) copy-start(bf16[320,3072]{1,0:T(8,128)(2,1)} %get-tuple-element.16.dy_ref) | copy-start | bytes 5898244
  52.3 35.5 %copy-start.1 = (bf16[320,1344]{1,0:T(8,128)(2,1)S(1)}, bf16[320,1344]{1,0:T(8,128)(2,1)}, u32[]{:S(2)}) copy-start(bf16[320,1344]{1,0:T(8,128)(2,1)} %get-tuple-element.15.scaled_ref) | copy-start | bytes 2580484

commit v3 on v2

--- a/solution.py
+++ b/solution.py
@@ -88,13 +88,14 @@
     to_core = [remote(block(j, t), block(j, t), core_send.at[j], core_recv.at[j], (e, core)) for j in range(n)]
     to_side = [remote(block(j, t), block(j, t), side_send.at[j], side_recv.at[j], (e, side)) for j in range(n)]
     passed = [remote(block(j, side), block(j, side), pass_send.at[j], pass_recv.at[j], (e, core)) for j in range(n)]
-    for j in range(n):
+    def forward(j):
         if j == 0:
             own.wait()
         else:
             remote(send_ref.at[others[j]], block(j, t), out_send.at[j], out_recv.at[j], (others[j], t)).wait_recv()
         to_side[j].start()
         to_core[j].start()
+
     slots = dy_ref.shape[0]
     hidden = gate_ref.shape[1]
     reach = 2 * width
@@ -103,61 +104,52 @@
     def half_columns(index):
         return pl.ds(pl.multiple_of(index * reach, 128), reach)
 
-    def assemble(index):
+    group = n // 2
+    group_rows = group * cap
+    here = e // group
+
+    def assemble(g, index):
         for c in range(2):
             cols = pl.ds(pl.multiple_of(index * reach + c * width, 128), width)
-
-            for k in range(n // 2):
-                first = rows[2 * k, :, cols].astype(jnp.float32)
-                second = rows[2 * k + 1, :, cols].astype(jnp.float32)
-                span = slice(2 * k * cap, 2 * (k + 1) * cap)
+            for k in range(group // 2):
+                source = g * group + 2 * k
+                first = rows[source, :, cols].astype(jnp.float32)
+                second = rows[source + 1, :, cols].astype(jnp.float32)
+                span = pl.ds(pl.multiple_of(source * cap, 16), 2 * cap)
                 x_rows[span, cols] = jnp.concatenate([first[:cap], second[:cap]], axis=0).astype(jnp.bfloat16)
                 dy_ref[span, cols] = jnp.concatenate([first[cap:], second[cap:]], axis=0).astype(jnp.bfloat16)
 
-    def multiply(m, index, fresh):
+    def multiply(m, g, index, fresh):
         cols = half_columns(index)
+        span = pl.ds(pl.multiple_of(g * group_rows, 16), group_rows)
         for low in range(0, hidden, 512):
             tile = slice(low, min(low + 512, hidden))
             part = lax.dot_general(
-                (dy_ref if m == 2 else x_rows)[:, cols],
+                (dy_ref if m == 2 else x_rows)[span, cols],
                 weights[m, tile, cols],
                 (((1,), (1,)), ((), ())),
                 preferred_element_type=jnp.float32,
             )
-            acc[m, :, tile] = part if fresh else acc[m, :, tile] + part
+            acc[m, span, tile] = part if fresh else acc[m, span, tile] + part
 
     def pass_on(k):
         remote(block(k, side), block(k, side), side_send.at[k], side_recv.at[k], (e, side)).wait_recv()
         passed[k].start()
 
-    for k in range(n // 2):
-        pass_on(k)
-    for j in range(n):
-        remote(block(j, core), block(j, core), core_send.at[j], core_recv.at[j], (e, core)).wait_recv()
-    assemble(near)
-    for m in range(3):
-        loads[m].wait()
-        multiply(m, near, True)
-        if m < 2:
-            pass_on(n // 2 + m)
-    for k in range(n // 2 + 2, n):
-        pass_on(k)
-    own_probs.wait()
-    for j in range(1, n):
-        remote(
-            probs_ref.at[others[j]], got_probs_ref.at[others[j]], prob_send.at[j], prob_recv.at[j], (others[j], t)
-        ).wait_recv()
-    for s in range(n):
-        prob_rows[s * cap : (s + 1) * cap, :] = got_probs_ref[s]
-    for j in range(n):
-        remote(block(j, far), block(j, far), pass_send.at[j], pass_recv.at[j], (e, core)).wait_recv()
-    assemble(1 - near)
-    for m in range(3):
-        multiply(m, 1 - near, False)
-
-    @pl.loop(0, slots // 16)
-    def _(r):
-        span = pl.ds(pl.multiple_of(r * 16, 16), 16)
+    def await_core(first, last):
+        for j in range(first, last):
+            remote(block(j, core), block(j, core), core_send.at[j], core_recv.at[j], (e, core)).wait_recv()
+
+    def await_far(first, last):
+        for j in range(first, last):
+            remote(block(j, far), block(j, far), pass_send.at[j], pass_recv.at[j], (e, core)).wait_recv()
+
+    def finish(g):
+        @pl.loop(0, group_rows // 16)
+        def _(r):
+            elementwise(pl.ds(pl.multiple_of(g * group_rows + r * 16, 16), 16))
+
+    def elementwise(span):
         prob = prob_rows[span, 0:1]
         score = jnp.zeros((16, 1), jnp.float32)
         for low in range(0, hidden, 384):
@@ -174,6 +166,45 @@
             gate_ref[span, tile] = (grad * pre_up * sigmoid * (1.0 + pre_gate * (1.0 - sigmoid))).astype(jnp.bfloat16)
             up_ref[span, tile] = (grad * silu).astype(jnp.bfloat16)
         score_rows[span, :] = jnp.broadcast_to(score, (16, 128))
+
+    for j in range(group):
+        forward(j)
+    await_core(0, group)
+    assemble(here, near)
+    for m in range(3):
+        loads[m].wait()
+        multiply(m, here, near, True)
+        if m < 2:
+            forward(group + m)
+    for k in range(group):
+        pass_on(k)
+    for j in range(group + 2, n):
+        forward(j)
+    await_far(0, group)
+    assemble(here, 1 - near)
+    for m in range(3):
+        multiply(m, here, 1 - near, False)
+    pass_on(group)
+    pass_on(group + 1)
+    own_probs.wait()
+    for j in range(1, n):
+        remote(
+            probs_ref.at[others[j]], got_probs_ref.at[others[j]], prob_send.at[j], prob_recv.at[j], (others[j], t)
+        ).wait_recv()
+    for s in range(n):
+        prob_rows[s * cap : (s + 1) * cap, :] = got_probs_ref[s]
+    finish(here)
+    for k in range(group + 2, n):
+        pass_on(k)
+    await_core(group, n)
+    assemble(1 - here, near)
+    for m in range(3):
+        multiply(m, 1 - here, near, True)
+    await_far(group, n)
+    assemble(1 - here, 1 - near)
+    for m in range(3):
+        multiply(m, 1 - here, 1 - near, False)
+    finish(1 - here)
 
     diagonal = lax.broadcasted_iota(jnp.int32, (cap, 128), 0) == lax.broadcasted_iota(jnp.int32, (cap, 128), 1)
     for s in range(n):

time: 95.4 us -> 95.9 us (level)
    pallas_call x1, Pallas kernels: 44.6 us -> 47.5 us  [dispatch(): pl.pallas_call(functools.partial(dispatch_kernel, n), out_shape=(jax.Shap...]
    pallas_call x1, Pallas kernels: 31.8 us -> 29.5 us  [combine(): pl.pallas_call(functools.partial(combine_kernel, n), out_shape=(jax.Shape...]
where the time goes in v3:
time: 95.9 us; the launch traced here: 95.5 us
  Pallas kernels  84.2 us (88%)
  other arithmetic  4.96 us (5%)
  matrix products  4.8 us (5%)
    pallas_call x1, Pallas kernels, dispatch(): pl.pallas_call(functools.partial(dispatch_kernel, n), out_shape=(jax.Shap...  47.5 us
    pallas_call x1, Pallas kernels, combine(): pl.pallas_call(functools.partial(combine_kernel, n), out_shape=(jax.Shape...  29.5 us
    pallas_call x1, Pallas kernels, down_product(): pl.pallas_call(down_kernel, grid=(full // tile,), out_shape=jax.ShapeDtyp...  7.19 us
    dot_general x1, matrix products, per_device(): jnp.dot(placer, jnp.concatenate([tokens, grad_out], axis=0), preferred_el...  2.32 us

profile of v3, /device:TPU:0, one launch (start us, length us, event | category | flops | bytes accessed | tf_op | source)
XLA Modules:
  0.0 95.5 jit_solution(10321193326661552257)
XLA Ops:
  0.6 0.7 convert_bitcast_fusion
  1.3 0.7 convert_reduce_fusion
  2.0 0.1 fusion.14
  2.1 0.7 select_reduce_fusion.1
  2.9 0.7 multiply_add_fusion.1
  3.5 0.7 broadcast_add_fusion
  4.2 0.1 pad_add_fusion
  4.3 1.0 %fusion.3.probs_ref = f32[8,40,128]{2,1,0:T(8,128)} fusion(f32[64]{0:T(128)S(1)} %get-tuple-element.26, s32[64]{0:T(128)S(1)} %get-tuple-element.22, f32[64]{0:T(128)S(1)} %get-tuple-element.27, s32[64]{0:T(128)S(1)} %get-tuple-element.23, f32[64]{0:T(128)S(1)} %get-tuple-element.28, s32[64]{0:T(128)S(1)} %get-tuple-element.24, ...), kind=kOutput, calls=%fused_computation.14 | convolution fusion | flops 5488640 | bytes 167168 | tf_op jit(solution)/shard_map/dot_general | solution.py:457
  5.3 2.3 %convolution_convert_fusion = bf16[640,768]{1,0:T(8,128)(2,1)} fusion(bf16[64,768]{1,0:T(8,128)(2,1)} %param.8, bf16[64,768]{1,0:T(8,128)(2,1)} %param.7, s32[128]{0:T(128)S(1)} %get-tuple-element.30, s32[128]{0:T(128)S(1)} %get-tuple-element.31, s32[128]{0:T(128)S(1)} %get-tuple-element.32, s32[128]{0:T(128)S(1)} %get-tuple-element.29), kind=kOutput, calls=%fused_computation | convolution fusion | flops 127696896 | bytes 1181696 | tf_op jit(solution)/shard_map/dot_general | solution.py:465
  7.6 47.5 %shard_map.94 = (bf16[320,3072]{1,0:T(8,128)(2,1)}, bf16[320,1344]{1,0:T(8,128)(2,1)}, bf16[320,1344]{1,0:T(8,128)(2,1)}, bf16[320,1344]{1,0:T(8,128)(2,1)}, f32[8,8,128]{2,1,0:T(8,128)}) custom-call(bf16[8,80,768]{2,1,0:T(8,128)(2,1)} %bitcast.39, f32[8,40,128]{2,1,0:T(8,128)} %fusion.3.probs_ref, bf16[1344,3072]{1,0:T(8,128)(2,1)} %bitcast.42, ...), custom_call_target="tpu_custom_call" | custom-call | flops 7927234560 | bytes 24772608 | tf_op jit(solution)/shard_map/pallas_call | solution.py:225
  55.1 0.0 copy-start
  55.1 0.0 copy-start.1
  55.1 29.5 %shard_map.95 = (bf16[8,80,384]{2,1,0:T(8,128)(2,1)}, f32[8,8,128]{2,1,0:T(8,128)}) custom-call(bf16[320,1344]{1,0:T(8,128)(2,1)} %get-tuple-element.10.gate_ref, bf16[320,1344]{1,0:T(8,128)(2,1)} %get-tuple-element.11.up_ref, f32[8,8,128]{2,1,0:T(8,128)} %get-tuple-element.12.score_ref, bf16[1344,3072]{1,0:T(8,128)(2,1)} %bitcast.43, ...), custom_call_target="tpu_custom_call" | custom-call | flops 5284823040 | bytes 16515072 | tf_op jit(solution)/shard_map/pallas_call | solution.py:375
  84.6 1.4 %convolution_convert_fusion.1 = bf16[128,384]{1,0:T(8,128)(2,1)S(1)} fusion(bf16[640,384]{1,0:T(8,128)(2,1)} %bitcast.46, s32[128]{0:T(128)S(1)} %get-tuple-element.30, s32[128]{0:T(128)S(1)} %get-tuple-element.31, s32[128]{0:T(128)S(1)} %get-tuple-element.32, s32[128]{0:T(128)S(1)} %get-tuple-element.29), kind=kOutput, calls=%fused_computation.1 | convolution fusion | flops 63946752 | bytes 591872 | tf_op jit(solution)/shard_map/dot_general | solution.py:474
  86.0 0.7 pad_maximum_fusion
  86.7 0.8 slice_reduce_fusion
  87.5 0.1 broadcast_in_dim.71
  87.5 0.8 select_reduce_fusion
  88.3 0.0 copy-done
  88.3 0.0 copy-done.1
  88.3 7.2 %shard_map.96 = bf16[1344,3072]{1,0:T(8,128)(2,1)} custom-call(bf16[320,1344]{1,0:T(8,128)(2,1)S(1)} %copy-done.1, bf16[320,3072]{1,0:T(8,128)(2,1)S(1)} %copy-done), custom_call_target="tpu_custom_call" | custom-call | flops 2642411520 | bytes 8257536 | tf_op jit(solution)/shard_map/pallas_call | solution.py:421
  (5 shorter events, 0.0 us)
Async XLA Ops:
  55.1 33.2 %copy-start = (bf16[320,3072]{1,0:T(8,128)(2,1)S(1)}, bf16[320,3072]{1,0:T(8,128)(2,1)}, u32[]{:S(2)}) copy-start(bf16[320,3072]{1,0:T(8,128)(2,1)} %get-tuple-element.16.dy_ref) | copy-start | bytes 5898244
  55.1 33.2 %copy-start.1 = (bf16[320,1344]{1,0:T(8,128)(2,1)S(1)}, bf16[320,1344]{1,0:T(8,128)(2,1)}, u32[]{:S(2)}) copy-start(bf16[320,1344]{1,0:T(8,128)(2,1)} %get-tuple-element.15.scaled_ref) | copy-start | bytes 2580484
